TPU v7x, 32 devices: a whole 2x2x4 slice. The times are simulated.
32 devices in a mesh: section: 4 (over z), ctx: 8 (over y, x, core).
Axes of the slice: x: 2, y: 2, z: 4, core: 2. Of those that a mesh axis runs over, the one named last changes fastest.
Arguments:
- queries: bfloat16 [4, 2048, 3072], P('section', 'ctx'), may hold values from -160 to 160
- keys: bfloat16 [4, 2048, 512], P('section', 'ctx'), may hold values from -48 to 48
- values: bfloat16 [4, 2048, 512], P('section', 'ctx'), may hold values from -15 to 15
- cotangent: bfloat16 [4, 2048, 3072], P('section', 'ctx'), may hold values from -6 to 6
- router_logits: bfloat16 [4, 2048], P('section', 'ctx'), may hold values from -8 to 8
- positions: int32 [4, 2048], P('section', 'ctx'), may hold values from -1 to 8191, as said below
- counts: int32 [4, 8], P('section', 'ctx'), may hold values from 0 to 2, as said below
Outputs:
- handed: bfloat16 [4, 2048, 3072], P('section', 'ctx')
- value_grad: bfloat16 [4, 2048, 512], P('section', 'ctx')
- gate_grad: bfloat16 [4, 2048], P('section', 'ctx')
Inputs may be any that keep to these rules, and one draw needn't show every extreme that they name: For every micro-batch and every shard c, the counts of shards 0 to c sum to c + 1 or c + 2; shard 0 holds 2 blocks; all counts of a micro-batch sum to 8. In shard c's slots, the first counts * 128 hold distinct positions in increasing order, all within c * 1024 to (c + 1) * 1024 - 1; the other slots hold -1.
All inputs are finite; a program needn't handle non-finite values.
Results may differ from a plain program's by a relative error of at most 0.0066.
Values may be sent and summed in bfloat16 or wider, within the bound.
No kernel may reach another device: no remote copies, remote signals or barrier semaphores. Data moves between devices by JAX's collectives and lax.ppermute only.
A program may use at most 128 MiB of HBM per device.

v0:
```python
import math

import jax
import jax.numpy as jnp
from jax import lax
from jax.sharding import PartitionSpec as P

QUERY_HEADS = 24
KEY_VALUE_HEADS = 4
HEAD_SIZE = 128
BLOCK_ROWS = 128
MAXB = 2


score_masked_out = -1e30


def carried_in(part, axis, combine, identity):
    place = lax.axis_index(axis)
    gathered = lax.all_gather(part, axis)
    state = jnp.zeros_like(part) + jnp.asarray(identity, part.dtype)

    def one(lap, state):
        return combine(state, lax.dynamic_index_in_dim(gathered, lap, 0, False))

    return lax.fori_loop(0, place, one, state)


def passed_along(block, axis, distance):
    devices = range(lax.axis_size(axis))
    route = [(i - distance, i) for i in devices if i - distance in devices]
    return lax.ppermute(block, axis, route)


def for_sending(x):

    def short(part):
        return part.astype(jnp.bfloat16) if part.dtype == jnp.float32 else part

    return jax.tree.map(short, x)


def from_behind(x, axis, by):
    devices = lax.axis_size(axis)
    return lax.ppermute(x, axis, [(i, (i + by) % devices) for i in range(devices)])


def add_ints(earlier, later):
    return earlier + later


def local(queries, keys, values, cotangent, router_logits, positions, counts):
    query_group_width = QUERY_HEADS // KEY_VALUE_HEADS
    shards = lax.axis_size("ctx")
    key_width = BLOCK_ROWS * min(shards, max(1, 512 // BLOCK_ROWS))
    score_scale = 1.0 / math.sqrt(HEAD_SIZE)
    blocks_held = counts[0, 0]
    before = carried_in(blocks_held - 1, "ctx", add_ints, jnp.int32(0))
    carried = before + blocks_held - 1
    last_block = jnp.maximum(blocks_held - 1, 0)
    own_arrays = (queries[0], keys[0], values[0], cotangent[0], router_logits[0], positions[0])
    outgoing = [
        lax.dynamic_slice_in_dim(source, last_block * BLOCK_ROWS, BLOCK_ROWS, 0)
        for source in own_arrays
    ]
    incoming = passed_along(
        (outgoing[0], outgoing[1], outgoing[2], outgoing[3], outgoing[4], outgoing[5]), "ctx", 1
    )
    received_one = before == 1
    chosen = [
        jnp.where(received_one, arriving, source[:BLOCK_ROWS])
        for arriving, source in zip(incoming, own_arrays)
    ]
    query_row_block, key_row_block, value_rows, grad_rows, logit_rows, place_rows = chosen
    gate_values = jax.nn.sigmoid(logit_rows.astype(jnp.float32))
    query_head_rows = query_row_block.reshape(
        BLOCK_ROWS, KEY_VALUE_HEADS, query_group_width, HEAD_SIZE
    )
    latest_query = jnp.max(place_rows)

    def split_width():
        return key_width

    def scores_for(key_portion, place_part):
        local_row_count = key_portion.shape[0]
        scores = (
            jnp.einsum(
                "qhgd,khd->hgqk",
                query_head_rows,
                key_portion.reshape(local_row_count, KEY_VALUE_HEADS, HEAD_SIZE),
                preferred_element_type=jnp.float32,
            )
            * score_scale
        )
        allowed = place_part[None, :] <= place_rows[:, None]
        return (scores, allowed)

    def absorb_part(running, key_portion, value_portion, place_part):
        row_top, weight_sum, summed = running
        local_row_count = key_portion.shape[0]
        scores, allowed = scores_for(key_portion, place_part)
        new_top = jnp.maximum(
            row_top, jnp.max(jnp.where(allowed, scores, score_masked_out), axis=-1)
        )
        weights = jnp.where(allowed, jnp.exp(scores - new_top[..., None]), 0.0)
        factor = jnp.exp(row_top - new_top)
        weight_sum = weight_sum * factor + jnp.sum(weights, axis=-1)
        summed = summed * factor[..., None] + jnp.einsum(
            "hgqk,khd->hgqd",
            weights.astype(jnp.bfloat16),
            value_portion.reshape(local_row_count, KEY_VALUE_HEADS, HEAD_SIZE),
            preferred_element_type=jnp.float32,
        )
        return (new_top, weight_sum, summed)

    def absorb(running, key_portion, value_portion, place_part):
        return lax.cond(
            jnp.min(place_part) > latest_query,
            lambda: running,
            lambda: absorb_part(running, key_portion, value_portion, place_part),
        )

    start_state = (
        jnp.full((KEY_VALUE_HEADS, query_group_width, BLOCK_ROWS), score_masked_out, jnp.float32),
        jnp.zeros((KEY_VALUE_HEADS, query_group_width, BLOCK_ROWS), jnp.float32),
        jnp.zeros((KEY_VALUE_HEADS, query_group_width, BLOCK_ROWS, HEAD_SIZE), jnp.float32),
    )
    collected_rows = (
        lax.all_gather(key_row_block, "ctx", axis=0, tiled=True),
        lax.all_gather(value_rows, "ctx", axis=0, tiled=True),
        lax.all_gather(for_sending(place_rows), "ctx", axis=0, tiled=True).astype(place_rows.dtype),
    )
    key_complete = collected_rows[0]
    local_row_count = key_complete.shape[0]
    rows_per_step = split_width()
    relay_step_count = local_row_count // rows_per_step
    stacked = (
        key_complete.reshape(relay_step_count, rows_per_step, KEY_VALUE_HEADS * HEAD_SIZE),
        collected_rows[1].reshape(relay_step_count, rows_per_step, KEY_VALUE_HEADS * HEAD_SIZE),
        collected_rows[2].reshape(relay_step_count, rows_per_step),
    )

    def visit(state_in, member):
        return (absorb(state_in, member[0], member[1], member[2]), None)

    final_state = lax.scan(visit, start_state, stacked)[0]
    row_top, weight_sum, summed = final_state
    attended = jnp.transpose(summed / weight_sum[..., None], (2, 0, 1, 3)).reshape(
        BLOCK_ROWS, QUERY_HEADS * HEAD_SIZE
    )
    log_total = row_top + jnp.log(weight_sum)
    gradient_broad = grad_rows.astype(jnp.float32)
    output_gradient = (
        (gate_values[:, None] * gradient_broad)
        .astype(jnp.bfloat16)
        .reshape(BLOCK_ROWS, KEY_VALUE_HEADS, query_group_width, HEAD_SIZE)
    )

    def value_portion(key_portion, place_part):
        local_row_count = key_portion.shape[0]
        scores, allowed = scores_for(key_portion, place_part)
        probabilities = jnp.where(allowed, jnp.exp(scores - log_total[..., None]), 0.0).astype(
            jnp.bfloat16
        )
        return jnp.einsum(
            "hgqk,qhgd->khd", probabilities, output_gradient, preferred_element_type=jnp.float32
        ).reshape(local_row_count, KEY_VALUE_HEADS * HEAD_SIZE)

    def value_block(key_portion, place_part):
        return lax.cond(
            jnp.min(place_part) > latest_query,
            lambda: jnp.zeros((key_portion.shape[0], KEY_VALUE_HEADS * HEAD_SIZE), jnp.float32),
            lambda: value_portion(key_portion, place_part),
        )

    key_portion = collected_rows[0]
    place_part = collected_rows[2]
    local_row_count = key_portion.shape[0]
    rows_per_step = split_width()
    relay_step_count = local_row_count // rows_per_step
    product_terms = lax.map(
        lambda member: value_block(member[0], member[1]),
        (
            key_portion.reshape(relay_step_count, rows_per_step, KEY_VALUE_HEADS * HEAD_SIZE),
            place_part.reshape(relay_step_count, rows_per_step),
        ),
    )
    value_sum = lax.psum_scatter(
        product_terms.reshape(local_row_count, KEY_VALUE_HEADS * HEAD_SIZE),
        "ctx",
        scatter_dimension=0,
        tiled=True,
    )
    branch = (gate_values[:, None] * attended).astype(jnp.bfloat16)
    gate_term = (
        gate_values * (1.0 - gate_values) * jnp.sum(gradient_broad * attended, axis=1)
    ).astype(jnp.bfloat16)
    value_finished = value_sum.astype(jnp.bfloat16)
    returned = passed_along((branch, value_finished, gate_term), "ctx", -1)
    local_results = (branch, value_finished, gate_term)
    slot_lists = ([], [], [])
    for slot_index in range(MAXB):
        local_slot = jnp.logical_and(before == 0, slot_index == 0)
        back_slot = jnp.logical_and(carried == 1, blocks_held - 1 == slot_index)
        for member_index in range(3):
            mine = local_results[member_index]
            filled = jnp.where(
                local_slot, mine, jnp.where(back_slot, returned[member_index], jnp.zeros_like(mine))
            )
            slot_lists[member_index].append(filled)
    owner_branch = jnp.concatenate(slot_lists[0], axis=0)
    value_grad = jnp.concatenate(slot_lists[1], axis=0)
    gate_grad = jnp.concatenate(slot_lists[2], axis=0)
    handed = from_behind(owner_branch, "section", 1)
    return (handed[None], value_grad[None], gate_grad[None])


def solution(mesh):
    return jax.shard_map(
        local,
        mesh=mesh,
        in_specs=(
            P("section", "ctx", None),
            P("section", "ctx", None),
            P("section", "ctx", None),
            P("section", "ctx", None),
            P("section", "ctx"),
            P("section", "ctx"),
            P("section", "ctx"),
        ),
        out_specs=(P("section", "ctx", None), P("section", "ctx", None), P("section", "ctx")),
        check_vma=False,
    )
```

profile of v0, /device:TPU:0, one launch (start us, length us, event | category | flops | bytes accessed | tf_op | source)
XLA Modules:
  0.0 184.8 jit_solution(6272222523864985987)
XLA Ops:
  8.8 2.4 %collective-permute-start.2 = (bf16[128,512]{1,0:T(8,128)(2,1)S(1)}, bf16[128,512]{1,0:T(8,128)(2,1)S(1)}, u32[]{:S(2)}, u32[]{:S(2)}) collective-permute-start(bf16[128,512]{1,0:T(8,128)(2,1)S(1)} %dynamic-slice_bitcast_fusion.1), channel_id=1, source_target_pairs={{0,1},{1,2},{2,3},{3,4},{4,5},{5,6},{6,7},{8,9},{9,10},{10,11},{11... | collective-permute-start | bytes 393224 | tf_op jit(solution)/shard_map/ppermute | solution.py:32
  11.2 1.2 dynamic-slice.6
  13.2 9.0 %all-reduce = s32[8]{0:T(128)S(1)} all-reduce(s32[8]{0:T(128)S(1)} %dynamic-update-slice), channel_id=1, replica_groups=mesh['section'=4,'ctx'=8] {'ctx'}, use_global_device_ids=true, to_apply=%add | all-reduce | flops 8 | bytes 64
  22.2 1.6 bitcast_select_fusion.4
  23.9 0.9 dynamic-slice_bitcast_fusion
  24.8 2.4 %collective-permute-start.4 = (bf16[128,512]{1,0:T(8,128)(2,1)S(1)}, bf16[128,512]{1,0:T(8,128)(2,1)S(1)}, u32[]{:S(2)}, u32[]{:S(2)}) collective-permute-start(bf16[128,512]{1,0:T(8,128)(2,1)S(1)} %dynamic-slice_bitcast_fusion), channel_id=1, source_target_pairs={{0,1},{1,2},{2,3},{3,4},{4,5},{5,6},{6,7},{8,9},{9,10},{10,11},{11... | collective-permute-start | bytes 393224 | tf_op jit(solution)/shard_map/ppermute | solution.py:32
  27.2 1.0 collective-permute-done.4
  28.2 1.6 bitcast_select_fusion.3
  29.8 2.1 %fusion.38 = (bf16[1,128,3072]{2,1,0:T(8,128)(2,1)S(1)}, bf16[1,128,3072]{2,1,0:T(8,128)(2,1)S(1)}, bf16[1,128,3072]{2,1,0:T(8,128)(2,1)S(1)}, bf16[1,128,3072]{2,1,0:T(8,128)(2,1)S(1)}) fusion(bf16[1,256,3072]{2,1,0:T(8,128)(2,1)} %param.20, s32[]{:T(128)S(6)} %select_n.127, bf16[1,256,3072]{2,1,0:T(8,128)(2,1)} %param.17), kind=kLoop, calls=%fused_computation.76 | loop fusion | bytes 6291460 | tf_op jit(solution)/shard_map/slice | solution.py:71
  31.9 1.2 copy.65
  33.1 6.8 %collective-permute-start.3 = (bf16[128,3072]{0,1:T(8,128)(2,1)}, bf16[128,3072]{0,1:T(8,128)(2,1)S(1)}, u32[]{:S(2)}, u32[]{:S(2)}) collective-permute-start(bf16[128,3072]{0,1:T(8,128)(2,1)} %bitcast.119), channel_id=1, source_target_pairs={{0,1},{1,2},{2,3},{3,4},{4,5},{5,6},{6,7},{8,9},{9,10},{10,11},{11... | collective-permute-start | bytes 2359304 | tf_op jit(solution)/shard_map/ppermute | solution.py:32
  39.9 4.3 %collective-permute-start.1 = (s32[128]{0:T(128)S(1)}, s32[128]{0:T(128)S(1)}, u32[]{:S(2)}, u32[]{:S(2)}) collective-permute-start(s32[128]{0:T(128)S(1)} %fusion.33), channel_id=1, source_target_pairs={{0,1},{1,2},{2,3},{3,4},{4,5},{5,6},{6,7},{8,9},{9,10},{10,11},{11... | collective-permute-start | bytes 1544 | tf_op jit(solution)/shard_map/ppermute | solution.py:32
  44.2 1.2 copy.71
  45.3 4.3 %collective-permute-start.7 = (bf16[128,3072]{0,1:T(8,128)(2,1)}, bf16[128,3072]{0,1:T(8,128)(2,1)}, u32[]{:S(2)}, u32[]{:S(2)}) collective-permute-start(bf16[128,3072]{0,1:T(8,128)(2,1)} %bitcast.118), channel_id=1, source_target_pairs={{0,1},{1,2},{2,3},{3,4},{4,5},{5,6},{6,7},{8,9},{9,10},{10,11},{11... | collective-permute-start | bytes 2359304 | tf_op jit(solution)/shard_map/ppermute | solution.py:32
  49.7 4.5 %collective-permute-start = (bf16[128]{0:T(256)(128)(2,1)S(1)}, bf16[128]{0:T(256)(128)(2,1)S(1)}, u32[]{:S(2)}, u32[]{:S(2)}) collective-permute-start(bf16[128]{0:T(256)(128)(2,1)S(1)} %fusion.32), channel_id=1, source_target_pairs={{0,1},{1,2},{2,3},{3,4},{4,5},{5,6},{6,7},{8,9},{9,10},{10,11},{11... | collective-permute-start | bytes 776 | tf_op jit(solution)/shard_map/ppermute | solution.py:32
  54.6 1.2 copy.92
  56.4 12.4 %all-gather = s32[8,1,128]{2,1,0:T(1,128)S(1)} all-gather(s32[1,1,128]{2,1,0:T(1,128)S(1)} %bitcast.122), channel_id=1, replica_groups=mesh['section'=4,'ctx'=8] {'ctx'}, dimensions={0}, use_global_device_ids=true | all-gather | bytes 4608 | tf_op jit(solution)/shard_map/all_gather | solution.py:131
  70.5 1.5 copy.67
  72.0 10.3 %all-gather.6.cloned.1.call-done = bf16[1024,512]{1,0:T(8,128)(2,1)} async-done(((bf16[128,512]{1,0:T(8,128)(2,1)}), bf16[1024,512]{1,0:T(8,128)(2,1)}) %all-gather.6.cloned.1.call-update) | async-done | bytes 1048592 | tf_op jit(solution)/shard_map/all_gather | solution.py:130
  82.3 1.5 copy.69
  83.8 1.3 broadcast_in_dim.68
  85.1 10.0 %while.35 = (s32[]{:T(128)}, f32[4,6,128]{2,1,0:T(8,128)S(1)}, f32[4,6,128]{2,1,0:T(8,128)S(1)}, f32[4,6,128,128]{3,2,1,0:T(8,128)}, s32[2,512]{1,0:T(2,128)S(1)...) while((s32[]{:T(128)}, f32[4,6,128]{2,1,0:T(8,128)S(1)}, ...), condition=%wide.region_9.10_spmd, body=%wide.region_3.9_spmd.sunk | while | flops 823466496 | bytes 39000888 | solution.py:146
  87.0 6.3 %conditional.4 = (f32[4,6,128]{2,1,0:T(8,128)S(1)}, f32[4,6,128]{2,1,0:T(8,128)S(1)}, f32[4,6,128,128]{3,2,1,0:T(8,128)}) conditional(s32[]{:T(128)} %convert_element_type.65, (s32[1,512]{1,0:T(1,128)S(1)}, s32[128]{0:T(128)S(1)}, bf16[2,512,512]{1,2,0:T(8,128)(2,1)S(1)}, s32[]{:T(128)}, bf16[128,4,6,128]{3,0,2,1:T(8,128)(2,1)S(1)}, ...), branch_computations={%region_5.7_spmd, %region_8.8_spmd} | conditional | flops 823465984 | bytes 38971988 | solution.py:117
  87.2 1.2 fusion
  88.4 1.3 fusion.4
  89.8 2.3 %multiply_add_fusion = f32[4,6,128,128]{3,2,1,0:T(8,128)S(1)} fusion(f32[4,6,128,128]{3,2,1,0:T(8,128)S(1)} %copy-done.2, bf16[512,4,128,1]{0,2,3,1:T(8,128)(2,1)S(1)} %bitcast.110, f32[4,512,128,6]{2,1,3,0:T(8,128)S(1)} %get-tuple-element.423, f32[4,6,128]{2,1,0:T(8,128)S(1)} %max.6, pred[128,512]{0,1:T(8,128)(4,1)S(1)} %broadcast_compare_fusion, ...), kind=kOutput, calls=%fused_computation.12 | convolution fusion | flops 409731072 | bytes 10051584 | tf_op jit(solution)/shard_map/while/body/eval_jaxpr/cond/branch_0_fun/hgqk,khd->hgqd/dot_general | solution.py:108
  92.1 1.1 copy-done.3
  95.2 1.9 %copy.70 = f32[4,6,128,128]{2,3,1,0:T(8,128)S(1)} copy(f32[4,6,128,128]{3,2,1,0:T(8,128)} %get-tuple-element.255) | data formatting | bytes 3145728 | tf_op jit(solution)/shard_map/while | solution.py:146
  97.3 1.0 copy-done.1
  98.9 1.7 fusion.25
  100.6 1.5 collective-permute-start.5
  102.1 14.7 %while.36 = (s32[]{:T(128)}, f32[2,512,512]{2,1,0:T(8,128)}, s32[2,512]{1,0:T(2,128)S(1)}, s32[]{:T(128)}, s32[128]{0:T(128)S(1)}, /*index=5*/bf16[2,512,512]{1,...) while((s32[]{:T(128)}, f32[2,512,512]{2,1,0:T(8,128)}, ...), condition=%wide.region_14.15_spmd, body=%wide.region_10.14_spmd.sunk | while | flops 811663872 | bytes 12733659 | solution.py:181
  103.9 3.7 %conditional.5 = (f32[1,512,512]{1,2,0:T(8,128)S(1)}) conditional(s32[]{:T(128)} %convert_element_type.66, (s32[1,512]{1,0:T(1,128)S(1)}, s32[128]{0:T(128)S(1)}, bf16[2,512,512]{1,2,0:T(8,128)(2,1)S(1)}, s32[]{:T(128)}, bf16[128,4,6,128]{3,0,2,1:T(8,128)(2,1)S(1)}, /*index=5*/f32[4,6,128]{2,1,0:T(8,128)S(1)}, ...), branch_computations={%region_12.12_spmd, %region_13.13_spmd} | conditional | flops 811663360 | bytes 4340236 | solution.py:170
  104.1 3.5 %fusion.18 = f32[4,512,128,1]{1,2,3,0:T(8,128)S(1)} fusion(bf16[128,4,6,128]{0,3,2,1:T(8,128)(2,1)} %get-tuple-element.235, f32[4,6,128]{2,1,0:T(8,128)S(1)} %get-tuple-element.234, pred[128,512]{0,1:T(8,128)(4,1)S(1)} %broadcast_compare_fusion.1, bf16[512,4,128,1]{0,2,3,1:T(8,128)(2,1)S(1)} %bitcast.111, bf16[128,4,6,128]{3,0,2,1:T(8,128)(2,1)S(1)} %get-tuple-element.233), kind=kOutput, calls=%fused_computation.25 | convolution fusion | flops 811597824 | bytes 3223552 | tf_op jit(solution)/shard_map/while/body/eval_jaxpr/cond/branch_0_fun/hgqk,qhgd->khd/dot_general | solution.py:165
  107.6 1.0 copy-done
  108.6 1.6 copy.95
  110.1 1.1 constant_dynamic-update-slice_fusion.2
  113.2 1.0 copy-done
  114.2 1.6 copy.95
  115.7 1.0 constant_dynamic-update-slice_fusion.2
  116.8 1.5 select_select_fusion
  118.5 1.5 collective-permute-start.6
  120.0 1.3 collective-permute-start.9
  121.3 50.6 %reduce-scatter.2.cloned.1.call-done = f32[128,512]{1,0:T(8,128)} async-done(((f32[1024,512]{1,0:T(8,128)}), f32[128,512]{1,0:T(8,128)}) %reduce-scatter.2.cloned.1.call-update) | async-done | bytes 262160 | tf_op jit(solution)/shard_map/reduce_scatter | solution.py:188
  171.9 1.0 convert_element_type.37
  172.9 1.3 collective-permute-start.8
  174.8 1.7 copy.76
  176.6 0.9 select_select_fusion.1
  (69 shorter events, 10.2 us)
Async XLA Ops:
  7.2 63.3 %all-gather.4.cloned.1.call-start = ((), (), s32[]{:S(2)}) async-start(), calls=%async_computation.1 | async-start | bytes 1179648 | tf_op jit(solution)/shard_map/all_gather | solution.py:129
  8.8 13.4 %collective-permute-start.2 = (bf16[128,512]{1,0:T(8,128)(2,1)S(1)}, bf16[128,512]{1,0:T(8,128)(2,1)S(1)}, u32[]{:S(2)}, u32[]{:S(2)}) collective-permute-start(bf16[128,512]{1,0:T(8,128)(2,1)S(1)} %dynamic-slice_bitcast_fusion.1), channel_id=1, source_target_pairs={{0,1},{1,2},{2,3},{3,4},{4,5},{5,6},{6,7},{8,9},{9,10},{10,11},{11... | collective-permute-start | bytes 393224 | tf_op jit(solution)/shard_map/ppermute | solution.py:32
  23.8 58.5 %all-gather.6.cloned.1.call-start = ((), (), s32[]{:S(2)}) async-start(), calls=%async_computation.2 | async-start | bytes 1179648 | tf_op jit(solution)/shard_map/all_gather | solution.py:130
  24.8 3.4 %collective-permute-start.4 = (bf16[128,512]{1,0:T(8,128)(2,1)S(1)}, bf16[128,512]{1,0:T(8,128)(2,1)S(1)}, u32[]{:S(2)}, u32[]{:S(2)}) collective-permute-start(bf16[128,512]{1,0:T(8,128)(2,1)S(1)} %dynamic-slice_bitcast_fusion), channel_id=1, source_target_pairs={{0,1},{1,2},{2,3},{3,4},{4,5},{5,6},{6,7},{8,9},{9,10},{10,11},{11... | collective-permute-start | bytes 393224 | tf_op jit(solution)/shard_map/ppermute | solution.py:32
  29.8 10.1 %copy-start.5 = (s32[1,256]{1,0:T(1,128)S(1)}, s32[1,256]{1,0:T(1,128)}, u32[]{:S(2)}) copy-start(s32[1,256]{1,0:T(1,128)} %param.22) | copy-start | bytes 3076
  29.8 142.1 %reduce-scatter.2.cloned.1.call-start = ((), (), s32[]{:S(2)}) async-start(), calls=%async_computation.3 | async-start | bytes 2359296 | tf_op jit(solution)/shard_map/reduce_scatter | solution.py:188
  31.9 17.8 %copy-start.6 = (bf16[1,256]{1,0:T(2,128)(2,1)S(1)}, bf16[1,256]{1,0:T(2,128)(2,1)}, u32[]{:S(2)}) copy-start(bf16[1,256]{1,0:T(2,128)(2,1)} %param.21) | copy-start | bytes 1540
  33.1 36.9 %collective-permute-start.3 = (bf16[128,3072]{0,1:T(8,128)(2,1)}, bf16[128,3072]{0,1:T(8,128)(2,1)S(1)}, u32[]{:S(2)}, u32[]{:S(2)}) collective-permute-start(bf16[128,3072]{0,1:T(8,128)(2,1)} %bitcast.119), channel_id=1, source_target_pairs={{0,1},{1,2},{2,3},{3,4},{4,5},{5,6},{6,7},{8,9},{9,10},{10,11},{11... | collective-permute-start | bytes 2359304 | tf_op jit(solution)/shard_map/ppermute | solution.py:32
  39.9 15.9 %collective-permute-start.1 = (s32[128]{0:T(128)S(1)}, s32[128]{0:T(128)S(1)}, u32[]{:S(2)}, u32[]{:S(2)}) collective-permute-start(s32[128]{0:T(128)S(1)} %fusion.33), channel_id=1, source_target_pairs={{0,1},{1,2},{2,3},{3,4},{4,5},{5,6},{6,7},{8,9},{9,10},{10,11},{11... | collective-permute-start | bytes 1544 | tf_op jit(solution)/shard_map/ppermute | solution.py:32
  45.3 51.9 %collective-permute-start.7 = (bf16[128,3072]{0,1:T(8,128)(2,1)}, bf16[128,3072]{0,1:T(8,128)(2,1)}, u32[]{:S(2)}, u32[]{:S(2)}) collective-permute-start(bf16[128,3072]{0,1:T(8,128)(2,1)} %bitcast.118), channel_id=1, source_target_pairs={{0,1},{1,2},{2,3},{3,4},{4,5},{5,6},{6,7},{8,9},{9,10},{10,11},{11... | collective-permute-start | bytes 2359304 | tf_op jit(solution)/shard_map/ppermute | solution.py:32
  49.7 49.1 %collective-permute-start = (bf16[128]{0:T(256)(128)(2,1)S(1)}, bf16[128]{0:T(256)(128)(2,1)S(1)}, u32[]{:S(2)}, u32[]{:S(2)}) collective-permute-start(bf16[128]{0:T(256)(128)(2,1)S(1)} %fusion.32), channel_id=1, source_target_pairs={{0,1},{1,2},{2,3},{3,4},{4,5},{5,6},{6,7},{8,9},{9,10},{10,11},{11... | collective-permute-start | bytes 776 | tf_op jit(solution)/shard_map/ppermute | solution.py:32
  88.4 1.4 copy-start.2
  92.1 1.1 copy-start.3
  97.1 1.1 copy-start.1
  100.6 16.2 %collective-permute-start.5 = (bf16[128,3072]{0,1:T(8,128)(2,1)}, bf16[128,3072]{0,1:T(8,128)(2,1)}, u32[]{:S(2)}, u32[]{:S(2)}) collective-permute-start(bf16[128,3072]{0,1:T(8,128)(2,1)} %get-tuple-element.437), channel_id=1, source_target_pairs={{1,0},{2,1},{3,2},{4,3},{5,4},{6,5},{7,6},{9,8},{10,9},{11,10},{12... | collective-permute-start | bytes 2359304 | tf_op jit(solution)/shard_map/ppermute | solution.py:32
  107.6 1.0 copy-start
  113.2 1.0 copy-start
  118.5 56.3 %collective-permute-start.6 = (bf16[256,3072]{0,1:T(8,128)(2,1)S(1)}, bf16[256,3072]{0,1:T(8,128)(2,1)S(1)}, u32[]{:S(2)}, u32[]{:S(2)}) collective-permute-start(bf16[256,3072]{0,1:T(8,128)(2,1)S(1)} %pad_maximum_fusion), channel_id=1, source_target_pairs={{0,8},{8,16},{16,24},{24,0},{1,9},{9,17},{17,25},{25,1},{2,10},{10... | collective-permute-start | bytes 4718600 | tf_op jit(solution)/shard_map/ppermute | solution.py:45
  120.0 54.2 %collective-permute-start.9 = (bf16[128]{0:T(256)(128)(2,1)S(1)}, bf16[128]{0:T(256)(128)(2,1)S(1)}, u32[]{:S(2)}, u32[]{:S(2)}) collective-permute-start(bf16[128]{0:T(256)(128)(2,1)S(1)} %get-tuple-element.418), channel_id=1, source_target_pairs={{1,0},{2,1},{3,2},{4,3},{5,4},{6,5},{7,6},{9,8},{10,9},{11,10},{12... | collective-permute-start | bytes 776 | tf_op jit(solution)/shard_map/ppermute | solution.py:32
  171.9 4.7 %copy-start.4 = (f32[128,512]{1,0:T(8,128)S(1)}, f32[128,512]{1,0:T(8,128)}, u32[]{:S(2)}) copy-start(f32[128,512]{1,0:T(8,128)} %reduce-scatter.2.cloned.1.call-done) | copy-start | bytes 786436
  172.9 3.6 %collective-permute-start.8 = (bf16[128,512]{1,0:T(8,128)(2,1)S(1)}, bf16[128,512]{1,0:T(8,128)(2,1)}, u32[]{:S(2)}, u32[]{:S(2)}) collective-permute-start(bf16[128,512]{1,0:T(8,128)(2,1)S(1)} %convert_element_type.37), channel_id=1, source_target_pairs={{1,0},{2,1},{3,2},{4,3},{5,4},{6,5},{7,6},{9,8},{10,9},{11,10},{12... | collective-permute-start | bytes 393224 | tf_op jit(solution)/shard_map/ppermute | solution.py:32
Sparse Core Ops, SparseCore 0:
  23.9 32.8 all-gather.3
  58.8 23.5 all-gather.5
  116.9 54.9 reduce-scatter.1
where the time goes:
time: 188 us; the launch traced here: 185 us
  waiting for transfers between devices  61.9 us (33%)
  starting transfers between devices  30.4 us (16%)
  local copies, waits for them, and re-layouts  28.8 us (15%)
  blocking collectives  21.4 us (11%)
  other arithmetic  15.5 us (8%)
  between operations  14.7 us (8%)
  matrix products  6.92 us (4%)
  loops' own time  5.1 us (3%)
    reduce_scatter x1, waiting for transfers between devices, local(): lax.psum_scatter(product_terms.reshape(local_row_count, KEY_VALUE_HEADS *...  50.6 us
    ppermute x9, starting transfers between devices, passed_along(): return lax.ppermute(block, axis, route)  28.7 us
    all_gather x1, blocking collectives, local(): lax.all_gather(for_sending(place_rows), 'ctx', axis=0, tiled=True)  12.4 us
    all_gather x1, waiting for transfers between devices, local(): lax.all_gather(value_rows, 'ctx', axis=0, tiled=True)  10.3 us
    unnamed x1, blocking collectives  9.05 us
    unnamed x14, local copies, waits for them, and re-layouts  6.23 us
    while x4, local copies, waits for them, and re-layouts, local(): final_state = lax.scan(visit, start_state, stacked)[0]  5.24 us
    dynamic_update_slice x4, local copies, waits for them, and re-layouts, local(): lax.map(lambda member: value_block(member[0], member[1]), (key_portion.re...  5.23 us
  transfers between devices with their start and end apart: 13, of which 3 were waited for; matrix products, arithmetic and copies ran while one was open for 22% of the time, Pallas kernels for 0%

commit v1 on v0

v1 whole, which is shorter than its diff:
```python
import math

import jax
import jax.numpy as jnp
from jax import lax
from jax.experimental import pallas as pl
from jax.experimental.pallas import tpu as pltpu
from jax.sharding import PartitionSpec as P

QUERY_HEADS = 24
KEY_VALUE_HEADS = 4
HEAD_SIZE = 128
BLOCK_ROWS = 128
MAXB = 2

CORES = 2
GROUP = QUERY_HEADS // KEY_VALUE_HEADS
LOCAL_HEADS = KEY_VALUE_HEADS // CORES
GROUP_WIDTH = GROUP * HEAD_SIZE
HALF_QUERY = LOCAL_HEADS * GROUP_WIDTH
HALF_KEY = LOCAL_HEADS * HEAD_SIZE
CHIP_BLOCKS = 2 * MAXB - 1
CHIP_ROWS = CHIP_BLOCKS * BLOCK_ROWS
META_ROWS = 16
SLOTS = MAXB * BLOCK_ROWS
MASKED = -1e30
VMEM_LIMIT = 48 * 1024 * 1024
f32 = jnp.float32
bf16 = jnp.bfloat16
i32 = jnp.int32
K_COL = HALF_QUERY
V_COL = HALF_QUERY + HALF_KEY
M_COL = HALF_QUERY + 2 * HALF_KEY
PAYLOAD = M_COL + HEAD_SIZE


def params():
    return pltpu.CompilerParams(vmem_limit_bytes=VMEM_LIMIT)


def whole(shape):
    return pl.BlockSpec(shape, lambda i, s: (0,) * len(shape))


def call(body, scalars, grid_in, operands, outs, out_specs, scratch=(), flops=0, moved=0):
    return pl.pallas_call(
        body,
        grid_spec=pltpu.PrefetchScalarGridSpec(
            num_scalar_prefetch=1,
            grid=(1,),
            in_specs=grid_in,
            out_specs=out_specs,
            scratch_shapes=list(scratch),
        ),
        out_shape=outs,
        compiler_params=params(),
        cost_estimate=pl.CostEstimate(flops=flops, bytes_accessed=moved, transcendentals=0),
    )(scalars, *operands)


def shape(rows, columns, kind=bf16):
    return jax.ShapeDtypeStruct((rows, columns), kind)


def rows_of(block):
    return pl.ds(pl.multiple_of(block * BLOCK_ROWS, BLOCK_ROWS), BLOCK_ROWS)


def pack_kernel(s, q, k, v, logits, out, column):
    count = s[1]
    for b in range(MAXB):
        row = logits[0:1, b * BLOCK_ROWS : (b + 1) * BLOCK_ROWS].astype(f32)
        tall = jnp.broadcast_to(row, (BLOCK_ROWS, BLOCK_ROWS)).T
        lane = lax.broadcasted_iota(i32, (BLOCK_ROWS, HEAD_SIZE), 1)
        meta = jnp.where(lane < HEAD_SIZE // 2, tall, count.astype(f32)).astype(bf16)
        rows = slice(b * BLOCK_ROWS, (b + 1) * BLOCK_ROWS)
        out[rows, M_COL:] = meta
        column[rows, :] = meta
    out[:, 0:HALF_QUERY] = q[...]
    out[:, K_COL:V_COL] = k[...]
    out[:, V_COL:M_COL] = v[...]


def as_scalar(x):
    return jnp.max(x.astype(f32)).astype(i32)


def chip_counts(s, meta):
    own = s[1]
    other = as_scalar(meta[0:META_ROWS, HEAD_SIZE // 2 :])
    first = jnp.where(s[0] == 0, own, other)
    return first, own + other


def place_of(block, first, core):
    on_first = block < first
    slot = jnp.where(on_first, block, block - first)
    mine = jnp.where(on_first, 0, 1) == core
    return mine, slot


def chip_kernel(s, k, v, kr, vr, meta, *outs):
    first, live = chip_counts(s, meta)
    for b in range(CHIP_BLOCKS):
        mine, slot = place_of(b, first, s[0])
        rows = slice(b * BLOCK_ROWS, (b + 1) * BLOCK_ROWS)

        def copy(keys, vals):
            for h in range(LOCAL_HEADS):
                cols = slice(h * HEAD_SIZE, (h + 1) * HEAD_SIZE)
                outs[h][rows, 0:HEAD_SIZE] = keys[rows_of(slot), cols]
                outs[h][rows, HEAD_SIZE:] = vals[rows_of(slot), cols]

        @pl.when(jnp.logical_and(b < live, mine))
        def _():
            copy(k, v)

        @pl.when(jnp.logical_and(b < live, jnp.logical_not(mine)))
        def _():
            copy(kr, vr)

        @pl.when(b >= live)
        def _():
            for h in range(LOCAL_HEADS):
                outs[h][rows, :] = jnp.zeros((BLOCK_ROWS, 2 * HEAD_SIZE), bf16)

    for h in range(LOCAL_HEADS):
        outs[h][CHIP_ROWS:, :] = jnp.broadcast_to(live.astype(f32), (META_ROWS, 2 * HEAD_SIZE)).astype(bf16)


def attend_kernel(chips, chunk, has_prior, s, *refs):
    q, qr, cot, cotr, column, columnr = refs[:6]
    at = 6
    kv = refs[at : at + chips]
    at += chips
    prior = refs[at : at + chips] if has_prior else None
    at += chips if has_prior else 0
    branch, gate_part = refs[at : at + 2]
    at += 2
    dvs = refs[at : at + chips]
    at += chips
    kd, vd, qs, og, scores, probs, top, acc, dv = refs[at:]

    first, live = chip_counts(s, columnr)
    core = s[0]
    ones = jnp.ones((BLOCK_ROWS, HEAD_SIZE), bf16)
    vd[...] = jnp.zeros_like(vd)
    dv[...] = jnp.zeros_like(dv)

    held = [live] + [as_scalar(kv[d][CHIP_ROWS:, 0:HEAD_SIZE]) for d in range(1, chips)]
    starts = [None] * chips
    position = jnp.int32(0)
    for d in list(range(1, chips)) + [0]:
        starts[d] = position
        for b in range(CHIP_BLOCKS):

            @pl.when(b < held[d])
            def _(d=d, b=b, position=position):
                rows = slice(b * BLOCK_ROWS, (b + 1) * BLOCK_ROWS)
                to = rows_of(position + b)
                kd[to, :] = kv[d][rows, 0:HEAD_SIZE]
                vd[to, 0:HEAD_SIZE] = kv[d][rows, HEAD_SIZE:]
                vd[to, HEAD_SIZE:] = ones

        position = position + held[d]
    base = starts[0]
    scale = math.log2(math.e) / math.sqrt(HEAD_SIZE)
    tall = GROUP * BLOCK_ROWS

    def part(j):
        return pl.ds(pl.multiple_of(j * chunk, chunk), chunk)

    def one_block(b, _):
        mine, slot = place_of(b, first, core)
        here = rows_of(slot)

        @pl.when(mine)
        def _():
            for i in range(GROUP):
                qs[i * BLOCK_ROWS : (i + 1) * BLOCK_ROWS, :] = q[here, i * HEAD_SIZE : (i + 1) * HEAD_SIZE]

        @pl.when(jnp.logical_not(mine))
        def _():
            for i in range(GROUP):
                qs[i * BLOCK_ROWS : (i + 1) * BLOCK_ROWS, :] = qr[here, i * HEAD_SIZE : (i + 1) * HEAD_SIZE]

        t = base + b
        last = t * BLOCK_ROWS // chunk

        def score(j):
            return lax.dot_general(
                qs[...], kd[part(j), :], (((1,), (1,)), ((), ())), preferred_element_type=f32
            )

        x = score(last)
        key = last * chunk + lax.broadcasted_iota(i32, (BLOCK_ROWS, chunk), 1)
        row = t * BLOCK_ROWS + lax.broadcasted_iota(i32, (BLOCK_ROWS, chunk), 0)
        allowed = key <= row
        x = jnp.where(allowed[None], x.reshape(GROUP, BLOCK_ROWS, chunk), MASKED).reshape(tall, chunk)
        scores[last] = x
        top[...] = jnp.max(x, axis=1, keepdims=True)

        def more(j, _):
            x = score(j)
            scores[j] = x
            top[...] = jnp.maximum(top[...], jnp.max(x, axis=1, keepdims=True))
            return 0

        lax.fori_loop(0, last, more, 0)
        acc[...] = jnp.zeros_like(acc)

        def weigh(j, _):
            p = jnp.exp2((scores[j] - top[...]) * scale).astype(bf16)
            probs[j] = p
            acc[...] += jnp.dot(p, vd[part(j), :], preferred_element_type=f32)
            return 0

        lax.fori_loop(0, last + 1, weigh, 0)

        def finish(grad, col):
            logit = jnp.broadcast_to(col[here, 0:1].astype(f32), (BLOCK_ROWS, HEAD_SIZE))
            gate = 1.0 / (1.0 + jnp.exp(-logit))
            total = jnp.zeros((BLOCK_ROWS, HEAD_SIZE), f32)
            for i in range(GROUP):
                rows = slice(i * BLOCK_ROWS, (i + 1) * BLOCK_ROWS)
                cols = slice(i * HEAD_SIZE, (i + 1) * HEAD_SIZE)
                inverse = 1.0 / acc[rows, HEAD_SIZE:]
                attended = acc[rows, 0:HEAD_SIZE] * inverse
                branch[rows_of(b), cols] = (gate * attended).astype(bf16)
                g = grad[here, cols].astype(f32)
                total = total + g * attended
                og[rows, :] = (gate * g * inverse).astype(bf16)
            gate_part[rows_of(b), :] = total

        @pl.when(mine)
        def _():
            finish(cot, column)

        @pl.when(jnp.logical_not(mine))
        def _():
            finish(cotr, columnr)

        def back(j, _):
            dv[part(j), :] += lax.dot_general(
                probs[j], og[...], (((0,), (0,)), ((), ())), preferred_element_type=f32
            )
            return 0

        lax.fori_loop(0, last + 1, back, 0)
        return 0

    lax.fori_loop(0, live, one_block, 0)

    for b in range(CHIP_BLOCKS):
        rows = slice(b * BLOCK_ROWS, (b + 1) * BLOCK_ROWS)

        @pl.when(b >= live)
        def _():
            branch[rows, :] = jnp.zeros((BLOCK_ROWS, GROUP_WIDTH), bf16)
            gate_part[rows, :] = jnp.zeros((BLOCK_ROWS, HEAD_SIZE), f32)

        for d in range(chips):
            cols = slice(0, HEAD_SIZE)
            if has_prior:
                dvs[d][rows, 0:HEAD_SIZE] = prior[d][rows, :]
                cols = slice(HEAD_SIZE, 2 * HEAD_SIZE)

            @pl.when(b < held[d])
            def _():
                dvs[d][rows, cols] = dv[rows_of(starts[d] + b), :].astype(dvs[d].dtype)

            @pl.when(b >= held[d])
            def _():
                dvs[d][rows, cols] = jnp.zeros((BLOCK_ROWS, HEAD_SIZE), dvs[d].dtype)

    lane = lax.broadcasted_iota(i32, (META_ROWS, GROUP_WIDTH), 1)
    branch[CHIP_ROWS:, :] = jnp.where(lane < HEAD_SIZE // 2, first.astype(f32), (live - first).astype(f32)).astype(bf16)


def spread(slot, core, first, second, write, clear):
    held = jnp.where(core == 0, first, second)
    block = jnp.where(core == 0, slot, first + slot)

    @pl.when(slot < held)
    def _():
        write(rows_of(jnp.minimum(block, CHIP_BLOCKS - 1)))

    @pl.when(slot >= held)
    def _():
        clear()


def branch_kernel(s, *refs):
    parts = refs[:LOCAL_HEADS]
    mine, theirs = refs[LOCAL_HEADS:]
    first = as_scalar(parts[0][CHIP_ROWS:, 0 : HEAD_SIZE // 2])
    second = as_scalar(parts[0][CHIP_ROWS:, HEAD_SIZE // 2 : HEAD_SIZE])
    for out, core in ((mine, s[0]), (theirs, 1 - s[0])):
        for slot in range(MAXB):
            rows = slice(slot * BLOCK_ROWS, (slot + 1) * BLOCK_ROWS)

            def write(source):
                for h in range(LOCAL_HEADS):
                    out[rows, h * GROUP_WIDTH : (h + 1) * GROUP_WIDTH] = parts[h][source, :]

            def clear():
                out[rows, :] = jnp.zeros((BLOCK_ROWS, HALF_QUERY), bf16)

            spread(slot, core, first, second, write, clear)


def join_kernel(s, mine, theirs, out):
    @pl.when(s[0] == 0)
    def _():
        out[:, 0:HALF_QUERY] = mine[...]
        out[:, HALF_QUERY:] = theirs[...]

    @pl.when(s[0] != 0)
    def _():
        out[:, 0:HALF_QUERY] = theirs[...]
        out[:, HALF_QUERY:] = mine[...]


def gradient_kernel(chips, s, *refs):
    columnr = refs[0]
    own = refs[1]
    arrived = refs[2 : 1 + chips]
    gate_parts = refs[1 + chips : 1 + chips + LOCAL_HEADS]
    mine, gate_mine, theirs = refs[1 + chips + LOCAL_HEADS :]
    first, live = chip_counts(s, columnr)
    second = live - first
    for which, core in ((0, s[0]), (1, 1 - s[0])):
        for slot in range(MAXB):
            rows = slice(slot * BLOCK_ROWS, (slot + 1) * BLOCK_ROWS)

            def write(source):
                total = own[source, :]
                for other in arrived:
                    total = total + other[source, :].astype(f32)
                summed = gate_parts[0][source, :]
                for h in range(1, LOCAL_HEADS):
                    summed = summed + gate_parts[h][source, :]
                summed = jnp.broadcast_to(jnp.sum(summed, axis=1, keepdims=True), (BLOCK_ROWS, HEAD_SIZE))
                if which == 0:
                    mine[rows, :] = total.astype(bf16)
                    gate_mine[rows, :] = summed
                else:
                    theirs[rows, 0:HALF_KEY] = total.astype(bf16)
                    high = summed.astype(bf16)
                    low = (summed - high.astype(f32)).astype(bf16)
                    lane = lax.broadcasted_iota(i32, (BLOCK_ROWS, HEAD_SIZE), 1)
                    theirs[rows, HALF_KEY:] = jnp.where(lane < HEAD_SIZE // 2, high, low)

            def clear():
                if which == 0:
                    mine[rows, :] = jnp.zeros((BLOCK_ROWS, HALF_KEY), bf16)
                    gate_mine[rows, :] = jnp.zeros((BLOCK_ROWS, HEAD_SIZE), f32)
                else:
                    theirs[rows, :] = jnp.zeros((BLOCK_ROWS, HALF_KEY + HEAD_SIZE), bf16)

            spread(slot, core, first, second, write, clear)


def finish_kernel(s, mine, gate_mine, theirs, column, out, gate_out):
    @pl.when(s[0] == 0)
    def _():
        out[:, 0:HALF_KEY] = mine[...]
        out[:, HALF_KEY:] = theirs[:, 0:HALF_KEY]

    @pl.when(s[0] != 0)
    def _():
        out[:, 0:HALF_KEY] = theirs[:, 0:HALF_KEY]
        out[:, HALF_KEY:] = mine[...]

    half = HALF_KEY + HEAD_SIZE // 2
    for b in range(MAXB):
        rows = slice(b * BLOCK_ROWS, (b + 1) * BLOCK_ROWS)
        total = (
            gate_mine[rows, 0:1]
            + theirs[rows, HALF_KEY : HALF_KEY + 1].astype(f32)
            + theirs[rows, half : half + 1].astype(f32)
        )
        logit = column[rows, 0:1].astype(f32)
        gate = 1.0 / (1.0 + jnp.exp(-logit))
        full = jnp.broadcast_to(gate * (1.0 - gate) * total, (BLOCK_ROWS, HEAD_SIZE)).T
        gate_out[0:1, rows] = full[0:1, :].astype(bf16)


def local(queries, keys, values, cotangent, router_logits, positions, counts):
    shards = lax.axis_size("ctx")
    sections = lax.axis_size("section")
    chips = shards // CORES
    core = lax.axis_index("ctx") % CORES
    scalars = jnp.stack([core.astype(i32), counts[0, 0]])
    q, k, v, cot = queries[0], keys[0], values[0], cotangent[0]

    def swap(x):
        return lax.ppermute(x, "ctx", [(i, i ^ 1) for i in range(shards)])

    def onward(x, by):
        step = by * CORES
        return lax.ppermute(x, "ctx", [(i, i + step) for i in range(shards) if 0 <= i + step < shards])

    def section_on(x):
        return lax.ppermute(x, "section", [(i, (i + 1) % sections) for i in range(sections)])

    def half_of(width, mine=True):
        return pl.BlockSpec((SLOTS, width), lambda i, s: (0, s[0] if mine else 1 - s[0]))

    def fixed(width, at):
        return pl.BlockSpec((SLOTS, width), lambda i, s: (0, at))

    column_spec = fixed(HEAD_SIZE, M_COL // HEAD_SIZE)
    payload, column = call(
        pack_kernel,
        scalars,
        [half_of(HALF_QUERY, False), half_of(HALF_KEY, False), half_of(HALF_KEY, False), whole((1, SLOTS))],
        (q, k, v, router_logits),
        (shape(SLOTS, PAYLOAD), shape(SLOTS, HEAD_SIZE)),
        (whole((SLOTS, PAYLOAD)), whole((SLOTS, HEAD_SIZE))),
        moved=2 * SLOTS * PAYLOAD * 2,
    )
    other = swap(payload)
    cot_other = swap(lax.dynamic_slice_in_dim(cot, (1 - core) * HALF_QUERY, HALF_QUERY, 1))
    packed_rows = CHIP_ROWS + META_ROWS
    packed = call(
        chip_kernel,
        scalars,
        [
            half_of(HALF_KEY),
            half_of(HALF_KEY),
            fixed(HALF_KEY, K_COL // HALF_KEY),
            fixed(HALF_KEY, V_COL // HALF_KEY),
            column_spec,
        ],
        (k, v, other, other, other),
        tuple(shape(packed_rows, 2 * HEAD_SIZE) for _ in range(LOCAL_HEADS)),
        tuple(whole((packed_rows, 2 * HEAD_SIZE)) for _ in range(LOCAL_HEADS)),
        moved=4 * packed_rows * HALF_KEY * 2,
    )
    gathered = [[packed[h]] + [onward(packed[h], d) for d in range(1, chips)] for h in range(LOCAL_HEADS)]

    chunk = min(4, shards) * BLOCK_ROWS
    steps = -(-shards * BLOCK_ROWS // chunk)
    reach = steps * chunk
    tall = GROUP * BLOCK_ROWS
    prior = []
    branches, gate_parts = [], []
    for h in range(LOCAL_HEADS):
        width = HEAD_SIZE * (2 if prior else 1)
        own_at = pl.BlockSpec((SLOTS, GROUP_WIDTH), lambda i, s, h=h: (0, s[0] * LOCAL_HEADS + h))
        results = call(
            lambda *refs, prior=bool(prior): attend_kernel(chips, chunk, prior, *refs),
            scalars,
            [own_at, fixed(GROUP_WIDTH, h), own_at, fixed(GROUP_WIDTH, h), whole((SLOTS, HEAD_SIZE)), column_spec]
            + [whole((packed_rows, 2 * HEAD_SIZE))] * chips
            + [whole((CHIP_ROWS, HEAD_SIZE)) for _ in prior],
            (q, other, cot, cot_other, column, other, *gathered[h], *prior),
            (shape(packed_rows, GROUP_WIDTH), shape(CHIP_ROWS, HEAD_SIZE, f32), shape(CHIP_ROWS, width, f32))
            + tuple(shape(CHIP_ROWS, width) for _ in range(chips - 1)),
            (whole((packed_rows, GROUP_WIDTH)), whole((CHIP_ROWS, HEAD_SIZE)))
            + (whole((CHIP_ROWS, width)),) * chips,
            scratch=(
                pltpu.VMEM((reach, HEAD_SIZE), bf16),
                pltpu.VMEM((reach, 2 * HEAD_SIZE), bf16),
                pltpu.VMEM((tall, HEAD_SIZE), bf16),
                pltpu.VMEM((tall, HEAD_SIZE), bf16),
                pltpu.VMEM((steps, tall, chunk), f32),
                pltpu.VMEM((steps, tall, chunk), bf16),
                pltpu.VMEM((tall, 1), f32),
                pltpu.VMEM((tall, 2 * HEAD_SIZE), f32),
                pltpu.VMEM((reach, HEAD_SIZE), f32),
            ),
            flops=12 * tall * HEAD_SIZE * reach,
            moved=6 * packed_rows * GROUP_WIDTH,
        )
        branches.append(section_on(results[0]))
        gate_parts.append(results[1])
        prior = results[2:]
    returned = [onward(prior[d], -d) for d in range(1, chips)]
    grad_mine, gate_mine, grad_theirs = call(
        lambda *refs: gradient_kernel(chips, *refs),
        scalars,
        [column_spec]
        + [whole((CHIP_ROWS, HALF_KEY))] * chips
        + [whole((CHIP_ROWS, HEAD_SIZE))] * LOCAL_HEADS,
        (other, prior[0], *returned, *gate_parts),
        (shape(SLOTS, HALF_KEY), shape(SLOTS, HEAD_SIZE, f32), shape(SLOTS, HALF_KEY + HEAD_SIZE)),
        (whole((SLOTS, HALF_KEY)), whole((SLOTS, HEAD_SIZE)), whole((SLOTS, HALF_KEY + HEAD_SIZE))),
        moved=8 * CHIP_ROWS * HALF_KEY,
    )
    grad_other = swap(grad_theirs)
    value_grad, gate_grad = call(
        finish_kernel,
        scalars,
        [
            whole((SLOTS, HALF_KEY)),
            whole((SLOTS, HEAD_SIZE)),
            whole((SLOTS, HALF_KEY + HEAD_SIZE)),
            whole((SLOTS, HEAD_SIZE)),
        ],
        (grad_mine, gate_mine, grad_other, column),
        (shape(SLOTS, CORES * HALF_KEY), shape(1, SLOTS)),
        (whole((SLOTS, CORES * HALF_KEY)), whole((1, SLOTS))),
        moved=8 * SLOTS * HALF_KEY,
    )
    branch_mine, branch_theirs = call(
        branch_kernel,
        scalars,
        [whole((packed_rows, GROUP_WIDTH))] * LOCAL_HEADS,
        tuple(branches),
        (shape(SLOTS, HALF_QUERY), shape(SLOTS, HALF_QUERY)),
        (whole((SLOTS, HALF_QUERY)), whole((SLOTS, HALF_QUERY))),
        moved=7 * SLOTS * HALF_QUERY,
    )
    branch_other = swap(branch_theirs)
    handed = call(
        join_kernel,
        scalars,
        [whole((SLOTS, HALF_QUERY))] * 2,
        (branch_mine, branch_other),
        shape(SLOTS, CORES * HALF_QUERY),
        whole((SLOTS, CORES * HALF_QUERY)),
        moved=8 * SLOTS * HALF_QUERY,
    )
    return (handed[None], value_grad[None], gate_grad)


def solution(mesh):
    rows = P("section", "ctx", None)
    flat = P("section", "ctx")
    return jax.shard_map(
        local,
        mesh=mesh,
        in_specs=(rows, rows, rows, rows, flat, flat, flat),
        out_specs=(rows, rows, flat),
        check_vma=False,
    )
```

time: 188 us -> 104 us (0.55); the launches traced: 185 us -> 105 us
  local copies, waits for them, and re-layouts: 28.8 us -> 5.18 us
  blocking collectives: 21.4 us -> 0 us
  Pallas kernels: 0 us -> 17.1 us
  other arithmetic: 15.5 us -> 0.08 us
  between operations: 14.7 us -> 1.48 us
  matrix products: 6.92 us -> 0 us
  starting transfers between devices: 30.4 us -> 24.6 us
  waiting for transfers between devices: 61.9 us -> 56.3 us
  loops' own time: 5.1 us -> 0 us
    ppermute x10 -> x15, waiting for transfers between devices: 0.98 us -> 56.3 us  [the longest x9 27.7 us: onward(): lax.ppermute(x, 'ctx', [(i, i + step) for i in range(shards) if 0 <= i +...]
    reduce_scatter x1 -> x0, waiting for transfers between devices: 50.6 us -> none  [local(): lax.psum_scatter(product_terms.reshape(local_row_count, KEY_VALUE_HEADS *...]
    pallas_call x0 -> x8, Pallas kernels: none -> 17.1 us  [call(): pl.pallas_call(body, grid_spec=pltpu.PrefetchScalarGridSpec(num_scalar_pr...]
    all_gather x1 -> x0, blocking collectives: 12.4 us -> none  [local(): lax.all_gather(for_sending(place_rows), 'ctx', axis=0, tiled=True)]
    all_gather x2 -> x0, waiting for transfers between devices: 10.4 us -> none  [the longest x1 10.3 us: local(): lax.all_gather(value_rows, 'ctx', axis=0, tiled=True)]
    unnamed x1 -> x0, blocking collectives: 9.05 us -> none
    while x10 -> x0, local copies, waits for them, and re-layouts: 7.18 us -> none  [the longest x4 5.24 us: local(): final_state = lax.scan(visit, start_state, stacked)[0]]
    dot_general x3 -> x0, matrix products: 6.92 us -> none  [the longest x1 3.45 us: value_portion(): jnp.einsum('hgqk,qhgd->khd', probabilities, output_gradient, preferred_el...]
  transfers between devices with their start and end apart: 13 -> 15, of which waited for: 3 -> 7; matrix products, arithmetic and copies ran while one was open for 22% -> 1% of each run, Pallas kernels for 0% -> 8%
where the time goes in v1:
time: 104 us; the launch traced here: 105 us
  waiting for transfers between devices  56.3 us (54%)
  starting transfers between devices  24.6 us (24%)
  Pallas kernels  17.1 us (16%)
  local copies, waits for them, and re-layouts  5.18 us (5%)
  between operations  1.48 us (1%)
    ppermute x9, waiting for transfers between devices, onward(): lax.ppermute(x, 'ctx', [(i, i + step) for i in range(shards) if 0 <= i +...  27.7 us
    ppermute x2, waiting for transfers between devices, section_on(): lax.ppermute(x, 'section', [(i, (i + 1) % sections) for i in range(sectio...  26.1 us
    ppermute x9, starting transfers between devices, onward(): lax.ppermute(x, 'ctx', [(i, i + step) for i in range(shards) if 0 <= i +...  17.3 us
    pallas_call x8, Pallas kernels, call(): pl.pallas_call(body, grid_spec=pltpu.PrefetchScalarGridSpec(num_scalar_pr...  17.1 us
    ppermute x2, starting transfers between devices, section_on(): lax.ppermute(x, 'section', [(i, (i + 1) % sections) for i in range(sectio...  6.55 us
    unnamed x14, local copies, waits for them, and re-layouts  4 us
    ppermute x4, waiting for transfers between devices, swap(): return lax.ppermute(x, 'ctx', [(i, i ^ 1) for i in range(shards)])  2.49 us
  transfers between devices with their start and end apart: 15, of which 7 were waited for; matrix products, arithmetic and copies ran while one was open for 1% of the time, Pallas kernels for 8%

profile of v1, /device:TPU:0, one launch (start us, length us, event | category | flops | bytes accessed | tf_op | source)
XLA Modules:
  0.0 104.8 jit_solution(2659621151536587282)
XLA Ops:
  1.3 0.1 pad_add_fusion.s.refs_0_
  1.4 1.4 %copy-done = bf16[1,256,3072]{2,1,0:T(8,128)(2,1)S(1)} copy-done((bf16[1,256,3072]{2,1,0:T(8,128)(2,1)S(1)}, bf16[1,256,3072]{2,1,0:T(8,128)(2,1)}, u32[]{:S(2)}) %copy-start) | copy-done | bytes 1572888
  2.8 0.9 copy-done.2
  3.7 0.9 copy-done.4
  4.7 0.7 copy-done.6
  5.4 0.6 shard_map.85
  6.0 0.5 collective-permute-start
  6.5 1.2 %dynamic-slice_bitcast_fusion = bf16[256,1536]{1,0:T(8,128)(2,1)S(1)} fusion(bf16[1,256,3072]{2,1,0:T(8,128)(2,1)} %param.10, s32[]{:T(128)S(6)} %select_n.11), kind=kLoop, calls=%fused_computation | loop fusion | bytes 1572868 | tf_op jit(solution)/shard_map/dynamic_slice | solution.py:424
  7.7 0.0 copy-start.1
  7.7 0.1 collective-permute-start.1
  7.8 1.1 %collective-permute-done.kr.vr.meta.refs_2_.refs_6_.refs_1_ = bf16[256,2176]{1,0:T(8,128)(2,1)S(1)} collective-permute-done((bf16[256,2176]{1,0:T(8,128)(2,1)S(1)}, bf16[256,2176]{1,0:T(8,128)(2,1)S(1)}, u32[]{:S(2)}, u32[]{:S(2)}) %collective-permute-start) | collective-permute-done | bytes 1114144 | tf_op jit(solution)/shard_map/ppermute | solution.py:398
  8.9 0.0 copy-done.3
  8.9 0.0 copy-done.5
  8.9 0.8 shard_map.86
  9.7 5.7 %collective-permute-start.4 = (bf16[400,256]{1,0:T(8,128)(2,1)S(1)}, bf16[400,256]{1,0:T(8,128)(2,1)S(1)}, u32[]{:S(2)}, u32[]{:S(2)}) collective-permute-start(bf16[400,256]{1,0:T(8,128)(2,1)S(1)} %get-tuple-element.28.refs_7_), channel_id=1, source_target_pairs={{0,6},{1,7},{8,14},{9,15},{16,22},{17,23},{24,30},{25,31}} | collective-permute-start | bytes 614408 | tf_op jit(solution)/shard_map/ppermute | solution.py:402
  15.4 1.3 %collective-permute-start.3 = (bf16[400,256]{1,0:T(8,128)(2,1)S(1)}, bf16[400,256]{1,0:T(8,128)(2,1)S(1)}, u32[]{:S(2)}, u32[]{:S(2)}) collective-permute-start(bf16[400,256]{1,0:T(8,128)(2,1)S(1)} %get-tuple-element.28.refs_7_), channel_id=1, source_target_pairs={{0,4},{1,5},{2,6},{3,7},{8,12},{9,13},{10,14},{11,15},{16,20},{17,... | collective-permute-start | bytes 614408 | tf_op jit(solution)/shard_map/ppermute | solution.py:402
  16.8 2.5 %collective-permute-start.2 = (bf16[400,256]{1,0:T(8,128)(2,1)S(1)}, bf16[400,256]{1,0:T(8,128)(2,1)S(1)}, u32[]{:S(2)}, u32[]{:S(2)}) collective-permute-start(bf16[400,256]{1,0:T(8,128)(2,1)S(1)} %get-tuple-element.28.refs_7_), channel_id=1, source_target_pairs={{0,2},{1,3},{2,4},{3,5},{4,6},{5,7},{8,10},{9,11},{10,12},{11,13},... | collective-permute-start | bytes 614408 | tf_op jit(solution)/shard_map/ppermute | solution.py:402
  19.2 1.3 %collective-permute-start.8 = (bf16[400,256]{1,0:T(8,128)(2,1)S(1)}, bf16[400,256]{1,0:T(8,128)(2,1)S(1)}, u32[]{:S(2)}, u32[]{:S(2)}) collective-permute-start(bf16[400,256]{1,0:T(8,128)(2,1)S(1)} %get-tuple-element.30.refs_7_), channel_id=1, source_target_pairs={{0,6},{1,7},{8,14},{9,15},{16,22},{17,23},{24,30},{25,31}} | collective-permute-start | bytes 614408 | tf_op jit(solution)/shard_map/ppermute | solution.py:402
  20.5 0.0 collective-permute-done.1.refs_4_
  20.6 1.3 %collective-permute-start.7 = (bf16[400,256]{1,0:T(8,128)(2,1)S(1)}, bf16[400,256]{1,0:T(8,128)(2,1)S(1)}, u32[]{:S(2)}, u32[]{:S(2)}) collective-permute-start(bf16[400,256]{1,0:T(8,128)(2,1)S(1)} %get-tuple-element.30.refs_7_), channel_id=1, source_target_pairs={{0,4},{1,5},{2,6},{3,7},{8,12},{9,13},{10,14},{11,15},{16,20},{17,... | collective-permute-start | bytes 614408 | tf_op jit(solution)/shard_map/ppermute | solution.py:402
  21.9 0.0 collective-permute-done.4.refs_10_
  21.9 1.3 %collective-permute-start.6 = (bf16[400,256]{1,0:T(8,128)(2,1)S(1)}, bf16[400,256]{1,0:T(8,128)(2,1)S(1)}, u32[]{:S(2)}, u32[]{:S(2)}) collective-permute-start(bf16[400,256]{1,0:T(8,128)(2,1)S(1)} %get-tuple-element.30.refs_7_), channel_id=1, source_target_pairs={{0,2},{1,3},{2,4},{3,5},{4,6},{5,7},{8,10},{9,11},{10,12},{11,13},... | collective-permute-start | bytes 614408 | tf_op jit(solution)/shard_map/ppermute | solution.py:402
  23.2 7.8 %collective-permute-done.3.refs_9_ = bf16[400,256]{1,0:T(8,128)(2,1)S(1)} collective-permute-done((bf16[400,256]{1,0:T(8,128)(2,1)S(1)}, bf16[400,256]{1,0:T(8,128)(2,1)S(1)}, u32[]{:S(2)}, u32[]{:S(2)}) %collective-permute-start.3) | collective-permute-done | bytes 204832 | tf_op jit(solution)/shard_map/ppermute | solution.py:402
  30.9 0.0 collective-permute-done.2.refs_8_
  30.9 0.0 copy-done.1
  30.9 5.3 %shard_map.87 = (bf16[400,768]{1,0:T(8,128)(2,1)S(1)}, f32[384,128]{1,0:T(8,128)S(1)}, f32[384,128]{1,0:T(8,128)S(1)}, bf16[384,128]{1,0:T(8,128)(2,1)S(1)}, bf1...) custom-call(s32[2]{0:T(128)S(1)} %pad_add_fusion.s.refs_0_, bf16[256,3072]{1,0:T(8,128)(2,1)S(1)} %bitcast.13, ...), custom_call_target="tpu_custom_call" | custom-call | flops 1207959552 | bytes 1843200 | tf_op jit(solution)/shard_map/pallas_call | solution.py:46
  36.2 0.0 collective-permute-done.8.refs_10_
  36.2 0.0 collective-permute-done.7.refs_9_
  36.3 0.0 collective-permute-done.6.refs_8_
  36.3 5.4 %shard_map.88 = (bf16[400,768]{1,0:T(8,128)(2,1)S(1)}, f32[384,128]{1,0:T(8,128)S(1)}, f32[384,256]{1,0:T(8,128)S(1)}, bf16[384,256]{1,0:T(8,128)(2,1)S(1)}, bf1...) custom-call(s32[2]{0:T(128)S(1)} %pad_add_fusion.s.refs_0_, bf16[256,3072]{1,0:T(8,128)(2,1)} %bitcast.11, ...), custom_call_target="tpu_custom_call" | custom-call | flops 1207959552 | bytes 1843200 | tf_op jit(solution)/shard_map/pallas_call | solution.py:46
  41.7 5.0 %collective-permute-start.9 = (bf16[400,768]{1,0:T(8,128)(2,1)S(1)}, bf16[400,768]{1,0:T(8,128)(2,1)S(1)}, u32[]{:S(2)}, u32[]{:S(2)}) collective-permute-start(bf16[400,768]{1,0:T(8,128)(2,1)S(1)} %get-tuple-element.35), channel_id=1, source_target_pairs={{0,8},{8,16},{16,24},{24,0},{1,9},{9,17},{17,25},{25,1},{2,10},{10... | collective-permute-start | bytes 1843208 | tf_op jit(solution)/shard_map/ppermute | solution.py:405
  46.7 1.6 %collective-permute-start.5 = (bf16[400,768]{1,0:T(8,128)(2,1)S(1)}, bf16[400,768]{1,0:T(8,128)(2,1)S(1)}, u32[]{:S(2)}, u32[]{:S(2)}) collective-permute-start(bf16[400,768]{1,0:T(8,128)(2,1)S(1)} %get-tuple-element.29), channel_id=1, source_target_pairs={{0,8},{8,16},{16,24},{24,0},{1,9},{9,17},{17,25},{25,1},{2,10},{10... | collective-permute-start | bytes 1843208 | tf_op jit(solution)/shard_map/ppermute | solution.py:405
  48.3 15.2 %collective-permute-done.9.refs_1_ = bf16[400,768]{1,0:T(8,128)(2,1)S(1)} collective-permute-done((bf16[400,768]{1,0:T(8,128)(2,1)S(1)}, bf16[400,768]{1,0:T(8,128)(2,1)S(1)}, u32[]{:S(2)}, u32[]{:S(2)}) %collective-permute-start.9) | collective-permute-done | bytes 614432 | tf_op jit(solution)/shard_map/ppermute | solution.py:405
  63.5 10.9 %collective-permute-done.5.refs_0_ = bf16[400,768]{1,0:T(8,128)(2,1)S(1)} collective-permute-done((bf16[400,768]{1,0:T(8,128)(2,1)S(1)}, bf16[400,768]{1,0:T(8,128)(2,1)S(1)}, u32[]{:S(2)}, u32[]{:S(2)}) %collective-permute-start.5) | collective-permute-done | bytes 614432 | tf_op jit(solution)/shard_map/ppermute | solution.py:405
  74.4 0.8 shard_map.89
  75.2 0.1 collective-permute-start.10
  75.3 1.3 %collective-permute-start.11 = (bf16[384,256]{1,0:T(8,128)(2,1)S(1)}, bf16[384,256]{1,0:T(8,128)(2,1)S(1)}, u32[]{:S(2)}, u32[]{:S(2)}) collective-permute-start(bf16[384,256]{1,0:T(8,128)(2,1)S(1)} %get-tuple-element.39), channel_id=1, source_target_pairs={{2,0},{3,1},{4,2},{5,3},{6,4},{7,5},{10,8},{11,9},{12,10},{13,11},... | collective-permute-start | bytes 589832 | tf_op jit(solution)/shard_map/ppermute | solution.py:402
  76.6 1.3 %collective-permute-start.12 = (bf16[384,256]{1,0:T(8,128)(2,1)S(1)}, bf16[384,256]{1,0:T(8,128)(2,1)S(1)}, u32[]{:S(2)}, u32[]{:S(2)}) collective-permute-start(bf16[384,256]{1,0:T(8,128)(2,1)S(1)} %get-tuple-element.40), channel_id=1, source_target_pairs={{4,0},{5,1},{6,2},{7,3},{12,8},{13,9},{14,10},{15,11},{20,16},{21,... | collective-permute-start | bytes 589832 | tf_op jit(solution)/shard_map/ppermute | solution.py:402
  77.9 1.3 %collective-permute-start.13 = (bf16[384,256]{1,0:T(8,128)(2,1)S(1)}, bf16[384,256]{1,0:T(8,128)(2,1)S(1)}, u32[]{:S(2)}, u32[]{:S(2)}) collective-permute-start(bf16[384,256]{1,0:T(8,128)(2,1)S(1)} %get-tuple-element.41), channel_id=1, source_target_pairs={{6,0},{7,1},{14,8},{15,9},{22,16},{23,17},{30,24},{31,25}} | collective-permute-start | bytes 589832 | tf_op jit(solution)/shard_map/ppermute | solution.py:402
  79.2 5.3 %collective-permute-done.11.refs_3_ = bf16[384,256]{1,0:T(8,128)(2,1)S(1)} collective-permute-done((bf16[384,256]{1,0:T(8,128)(2,1)S(1)}, bf16[384,256]{1,0:T(8,128)(2,1)S(1)}, u32[]{:S(2)}, u32[]{:S(2)}) %collective-permute-start.11) | collective-permute-done | bytes 196640 | tf_op jit(solution)/shard_map/ppermute | solution.py:402
  84.5 14.7 %collective-permute-done.12.refs_4_ = bf16[384,256]{1,0:T(8,128)(2,1)S(1)} collective-permute-done((bf16[384,256]{1,0:T(8,128)(2,1)S(1)}, bf16[384,256]{1,0:T(8,128)(2,1)S(1)}, u32[]{:S(2)}, u32[]{:S(2)}) %collective-permute-start.12) | collective-permute-done | bytes 196640 | tf_op jit(solution)/shard_map/ppermute | solution.py:402
  99.1 0.0 collective-permute-done.13.refs_5_
  99.1 1.0 shard_map.91
  100.1 0.1 collective-permute-start.14
  100.2 1.4 %collective-permute-done.14.theirs = bf16[256,384]{1,0:T(8,128)(2,1)S(1)} collective-permute-done((bf16[256,384]{1,0:T(8,128)(2,1)S(1)}, bf16[256,384]{1,0:T(8,128)(2,1)S(1)}, u32[]{:S(2)}, u32[]{:S(2)}) %collective-permute-start.14) | collective-permute-done | bytes 196640 | tf_op jit(solution)/shard_map/ppermute | solution.py:398
  101.6 1.4 %shard_map.92 = (bf16[256,512]{1,0:T(8,128)(2,1)}, bf16[1,256]{1,0:T(2,128)(2,1)}) custom-call(s32[2]{0:T(128)S(1)} %pad_add_fusion.s.refs_0_, bf16[256,256]{1,0:T(8,128)(2,1)S(1)} %get-tuple-element.44.mine, f32[256,128]{1,0:T(8,128)S(1)} %get-tuple-element.45.gate_mine, bf16[256,384]{1,0:T(8,128)(2,1)S(1)} %collective-permute-done.14.theirs, ...), custom_call_target="tpu_custom_call" | custom-call | bytes 524288 | tf_op jit(solution)/shard_map/pallas_call | solution.py:46
  103.0 0.0 collective-permute-done.10.theirs
  103.0 1.8 %shard_map.90 = bf16[256,3072]{1,0:T(8,128)(2,1)} custom-call(s32[2]{0:T(128)S(1)} %pad_add_fusion.s.refs_0_, bf16[256,1536]{1,0:T(8,128)(2,1)S(1)} %get-tuple-element.36.mine, bf16[256,1536]{1,0:T(8,128)(2,1)S(1)} %collective-permute-done.10.theirs), custom_call_target="tpu_custom_call" | custom-call | bytes 3145728 | tf_op jit(solution)/shard_map/pallas_call | solution.py:46
  (6 shorter events, 0.0 us)
Async XLA Ops:
  1.4 1.4 %copy-start = (bf16[1,256,3072]{2,1,0:T(8,128)(2,1)S(1)}, bf16[1,256,3072]{2,1,0:T(8,128)(2,1)}, u32[]{:S(2)}) copy-start(bf16[1,256,3072]{2,1,0:T(8,128)(2,1)} %param.7) | copy-start | bytes 4718596
  2.8 0.9 copy-start.2
  3.7 0.9 copy-start.4
  4.7 0.7 copy-start.6
  5.3 3.6 %copy-start.3 = (bf16[1,256,512]{2,1,0:T(8,128)(2,1)S(1)}, bf16[1,256,512]{2,1,0:T(8,128)(2,1)}, u32[]{:S(2)}) copy-start(bf16[1,256,512]{2,1,0:T(8,128)(2,1)} %param.8) | copy-start | bytes 786436
  5.4 3.6 %copy-start.5 = (bf16[1,256,512]{2,1,0:T(8,128)(2,1)S(1)}, bf16[1,256,512]{2,1,0:T(8,128)(2,1)}, u32[]{:S(2)}) copy-start(bf16[1,256,512]{2,1,0:T(8,128)(2,1)} %param.9) | copy-start | bytes 786436
  6.0 2.9 %collective-permute-start = (bf16[256,2176]{1,0:T(8,128)(2,1)S(1)}, bf16[256,2176]{1,0:T(8,128)(2,1)S(1)}, u32[]{:S(2)}, u32[]{:S(2)}) collective-permute-start(bf16[256,2176]{1,0:T(8,128)(2,1)S(1)} %get-tuple-element.26), channel_id=1, source_target_pairs={{0,1},{1,0},{2,3},{3,2},{4,5},{5,4},{6,7},{7,6},{8,9},{9,8},{10,11... | collective-permute-start | bytes 3342344 | tf_op jit(solution)/shard_map/ppermute | solution.py:398
  7.7 23.2 %copy-start.1 = (bf16[1,256,3072]{2,1,0:T(8,128)(2,1)S(1)}, bf16[1,256,3072]{2,1,0:T(8,128)(2,1)}, u32[]{:S(2)}) copy-start(bf16[1,256,3072]{2,1,0:T(8,128)(2,1)} %param.7) | copy-start | bytes 4718596
  7.7 12.8 %collective-permute-start.1 = (bf16[256,1536]{1,0:T(8,128)(2,1)S(1)}, bf16[256,1536]{1,0:T(8,128)(2,1)S(1)}, u32[]{:S(2)}, u32[]{:S(2)}) collective-permute-start(bf16[256,1536]{1,0:T(8,128)(2,1)S(1)} %dynamic-slice_bitcast_fusion), channel_id=1, source_target_pairs={{0,1},{1,0},{2,3},{3,2},{4,5},{5,4},{6,7},{7,6},{8,9},{9,8},{10,11... | collective-permute-start | bytes 2359304 | tf_op jit(solution)/shard_map/ppermute | solution.py:398
  9.7 12.1 %collective-permute-start.4 = (bf16[400,256]{1,0:T(8,128)(2,1)S(1)}, bf16[400,256]{1,0:T(8,128)(2,1)S(1)}, u32[]{:S(2)}, u32[]{:S(2)}) collective-permute-start(bf16[400,256]{1,0:T(8,128)(2,1)S(1)} %get-tuple-element.28.refs_7_), channel_id=1, source_target_pairs={{0,6},{1,7},{8,14},{9,15},{16,22},{17,23},{24,30},{25,31}} | collective-permute-start | bytes 614408 | tf_op jit(solution)/shard_map/ppermute | solution.py:402
  15.4 15.5 %collective-permute-start.3 = (bf16[400,256]{1,0:T(8,128)(2,1)S(1)}, bf16[400,256]{1,0:T(8,128)(2,1)S(1)}, u32[]{:S(2)}, u32[]{:S(2)}) collective-permute-start(bf16[400,256]{1,0:T(8,128)(2,1)S(1)} %get-tuple-element.28.refs_7_), channel_id=1, source_target_pairs={{0,4},{1,5},{2,6},{3,7},{8,12},{9,13},{10,14},{11,15},{16,20},{17,... | collective-permute-start | bytes 614408 | tf_op jit(solution)/shard_map/ppermute | solution.py:402
  16.8 14.2 %collective-permute-start.2 = (bf16[400,256]{1,0:T(8,128)(2,1)S(1)}, bf16[400,256]{1,0:T(8,128)(2,1)S(1)}, u32[]{:S(2)}, u32[]{:S(2)}) collective-permute-start(bf16[400,256]{1,0:T(8,128)(2,1)S(1)} %get-tuple-element.28.refs_7_), channel_id=1, source_target_pairs={{0,2},{1,3},{2,4},{3,5},{4,6},{5,7},{8,10},{9,11},{10,12},{11,13},... | collective-permute-start | bytes 614408 | tf_op jit(solution)/shard_map/ppermute | solution.py:402
  19.2 17.0 %collective-permute-start.8 = (bf16[400,256]{1,0:T(8,128)(2,1)S(1)}, bf16[400,256]{1,0:T(8,128)(2,1)S(1)}, u32[]{:S(2)}, u32[]{:S(2)}) collective-permute-start(bf16[400,256]{1,0:T(8,128)(2,1)S(1)} %get-tuple-element.30.refs_7_), channel_id=1, source_target_pairs={{0,6},{1,7},{8,14},{9,15},{16,22},{17,23},{24,30},{25,31}} | collective-permute-start | bytes 614408 | tf_op jit(solution)/shard_map/ppermute | solution.py:402
  20.6 15.7 %collective-permute-start.7 = (bf16[400,256]{1,0:T(8,128)(2,1)S(1)}, bf16[400,256]{1,0:T(8,128)(2,1)S(1)}, u32[]{:S(2)}, u32[]{:S(2)}) collective-permute-start(bf16[400,256]{1,0:T(8,128)(2,1)S(1)} %get-tuple-element.30.refs_7_), channel_id=1, source_target_pairs={{0,4},{1,5},{2,6},{3,7},{8,12},{9,13},{10,14},{11,15},{16,20},{17,... | collective-permute-start | bytes 614408 | tf_op jit(solution)/shard_map/ppermute | solution.py:402
  21.9 14.4 %collective-permute-start.6 = (bf16[400,256]{1,0:T(8,128)(2,1)S(1)}, bf16[400,256]{1,0:T(8,128)(2,1)S(1)}, u32[]{:S(2)}, u32[]{:S(2)}) collective-permute-start(bf16[400,256]{1,0:T(8,128)(2,1)S(1)} %get-tuple-element.30.refs_7_), channel_id=1, source_target_pairs={{0,2},{1,3},{2,4},{3,5},{4,6},{5,7},{8,10},{9,11},{10,12},{11,13},... | collective-permute-start | bytes 614408 | tf_op jit(solution)/shard_map/ppermute | solution.py:402
  41.7 21.8 %collective-permute-start.9 = (bf16[400,768]{1,0:T(8,128)(2,1)S(1)}, bf16[400,768]{1,0:T(8,128)(2,1)S(1)}, u32[]{:S(2)}, u32[]{:S(2)}) collective-permute-start(bf16[400,768]{1,0:T(8,128)(2,1)S(1)} %get-tuple-element.35), channel_id=1, source_target_pairs={{0,8},{8,16},{16,24},{24,0},{1,9},{9,17},{17,25},{25,1},{2,10},{10... | collective-permute-start | bytes 1843208 | tf_op jit(solution)/shard_map/ppermute | solution.py:405
  46.7 27.7 %collective-permute-start.5 = (bf16[400,768]{1,0:T(8,128)(2,1)S(1)}, bf16[400,768]{1,0:T(8,128)(2,1)S(1)}, u32[]{:S(2)}, u32[]{:S(2)}) collective-permute-start(bf16[400,768]{1,0:T(8,128)(2,1)S(1)} %get-tuple-element.29), channel_id=1, source_target_pairs={{0,8},{8,16},{16,24},{24,0},{1,9},{9,17},{17,25},{25,1},{2,10},{10... | collective-permute-start | bytes 1843208 | tf_op jit(solution)/shard_map/ppermute | solution.py:405
  75.2 27.8 %collective-permute-start.10 = (bf16[256,1536]{1,0:T(8,128)(2,1)S(1)}, bf16[256,1536]{1,0:T(8,128)(2,1)S(1)}, u32[]{:S(2)}, u32[]{:S(2)}) collective-permute-start(bf16[256,1536]{1,0:T(8,128)(2,1)S(1)} %get-tuple-element.37), channel_id=1, source_target_pairs={{0,1},{1,0},{2,3},{3,2},{4,5},{5,4},{6,7},{7,6},{8,9},{9,8},{10,11... | collective-permute-start | bytes 2359304 | tf_op jit(solution)/shard_map/ppermute | solution.py:398
  75.3 9.2 %collective-permute-start.11 = (bf16[384,256]{1,0:T(8,128)(2,1)S(1)}, bf16[384,256]{1,0:T(8,128)(2,1)S(1)}, u32[]{:S(2)}, u32[]{:S(2)}) collective-permute-start(bf16[384,256]{1,0:T(8,128)(2,1)S(1)} %get-tuple-element.39), channel_id=1, source_target_pairs={{2,0},{3,1},{4,2},{5,3},{6,4},{7,5},{10,8},{11,9},{12,10},{13,11},... | collective-permute-start | bytes 589832 | tf_op jit(solution)/shard_map/ppermute | solution.py:402
  76.6 22.5 %collective-permute-start.12 = (bf16[384,256]{1,0:T(8,128)(2,1)S(1)}, bf16[384,256]{1,0:T(8,128)(2,1)S(1)}, u32[]{:S(2)}, u32[]{:S(2)}) collective-permute-start(bf16[384,256]{1,0:T(8,128)(2,1)S(1)} %get-tuple-element.40), channel_id=1, source_target_pairs={{4,0},{5,1},{6,2},{7,3},{12,8},{13,9},{14,10},{15,11},{20,16},{21,... | collective-permute-start | bytes 589832 | tf_op jit(solution)/shard_map/ppermute | solution.py:402
  77.9 21.2 %collective-permute-start.13 = (bf16[384,256]{1,0:T(8,128)(2,1)S(1)}, bf16[384,256]{1,0:T(8,128)(2,1)S(1)}, u32[]{:S(2)}, u32[]{:S(2)}) collective-permute-start(bf16[384,256]{1,0:T(8,128)(2,1)S(1)} %get-tuple-element.41), channel_id=1, source_target_pairs={{6,0},{7,1},{14,8},{15,9},{22,16},{23,17},{30,24},{31,25}} | collective-permute-start | bytes 589832 | tf_op jit(solution)/shard_map/ppermute | solution.py:402
  100.1 1.5 %collective-permute-start.14 = (bf16[256,384]{1,0:T(8,128)(2,1)S(1)}, bf16[256,384]{1,0:T(8,128)(2,1)S(1)}, u32[]{:S(2)}, u32[]{:S(2)}) collective-permute-start(bf16[256,384]{1,0:T(8,128)(2,1)S(1)} %get-tuple-element.46), channel_id=1, source_target_pairs={{0,1},{1,0},{2,3},{3,2},{4,5},{5,4},{6,7},{7,6},{8,9},{9,8},{10,11... | collective-permute-start | bytes 589832 | tf_op jit(solution)/shard_map/ppermute | solution.py:398
